TPU v7x, 32 devices: a whole 2x2x4 slice. The times are simulated.
32 devices in a mesh: band: 2 (over y), row: 4 (over x, core), col: 4 (over z).
Axes of the slice: x: 2, y: 2, z: 4, core: 2. Of those that a mesh axis runs over, the one named last changes fastest.
Arguments:
- orbitals: bfloat16 [64, 64, 64, 128], P('band', 'row', 'col'), may hold values from -6 to 6
- band_ranking: int32 [2, 32], P('band'), may hold values from 0 to 31, each once within a row
- pool_states: bfloat16 [8, 64, 64, 128], P(None, 'row', 'col'), may hold values from -6 to 6
- state_order: int32 [8], replicated, may hold values from 0 to 7, each once
- gvector_index: int32 [24576], replicated, may hold values from 0 to 524287, as said below
- screened: bfloat16 [2, 24576, 24576], P(None, ('band', 'row'), 'col'), may hold values from -0.00024414062 to 0.00024414062
Outputs:
- sigma: float32 [2, 2, 2, 32], replicated
Inputs may be any that keep to these rules, and one draw needn't show every extreme that they name: `band_ranking`: each row holds every number of 0 to 31 once. `state_order`: holds every number of 0 to 7 once. `gvector_index`: 24576 distinct flat indices (kx 64 + ky) * 128 + kz into the transform grid.
All inputs are finite; a program needn't handle non-finite values.
Results may differ from a plain program's by a relative error of at most 0.0059.
Values may be sent and summed in bfloat16 or wider, within the bound.
A program may use at most 192 MiB of HBM per device.

v0:
```python
import math

import jax
import jax.numpy as jnp
from jax import lax
from jax.sharding import PartitionSpec as P

NX = 64
NY = 64
NZ = 128
GB = 16
NQ = 2


def real_table(length):
    indices = jnp.arange(length, dtype=jnp.int32)
    angles = (indices[:, None] * indices[None, :] % length).astype(jnp.float32) * (
        2.0 * math.pi / length
    )
    return jnp.stack([jnp.cos(angles), -jnp.sin(angles)])


def complex_table(length):
    indices = jnp.arange(length, dtype=jnp.int32)
    angles = (indices[:, None] * indices[None, :] % length).astype(jnp.float32) * (
        2.0 * math.pi / length
    )
    cosine_table = jnp.cos(angles)
    sine_table = jnp.sin(angles)
    return jnp.stack(
        [jnp.stack([cosine_table, -sine_table]), jnp.stack([sine_table, cosine_table])]
    )


def quadratic(left_pairs, right_pairs, sign_real, sign_imag):
    highest = lax.Precision.HIGHEST
    real_part = jnp.einsum(
        "mnr,mkr->nkm", left_pairs[:, :, 0], right_pairs[:, :, 0], precision=highest
    ) + sign_real * jnp.einsum(
        "mnr,mkr->nkm", left_pairs[:, :, 1], right_pairs[:, :, 1], precision=highest
    )
    imag_part = jnp.einsum(
        "mnr,mkr->nkm", left_pairs[:, :, 0], right_pairs[:, :, 1], precision=highest
    ) + sign_imag * jnp.einsum(
        "mnr,mkr->nkm", left_pairs[:, :, 1], right_pairs[:, :, 0], precision=highest
    )
    return jnp.stack([real_part, imag_part])


def body(orbitals, band_ranking, pool_states, state_order, gvector_index, screened):
    accurate = lax.Precision.HIGH
    x_local = orbitals.shape[1]
    y_local = orbitals.shape[2]
    row_devices = lax.axis_size("row")
    col_devices = lax.axis_size("col")
    pair_count = GB * NQ
    per_device = pair_count // (row_devices * col_devices)
    window = jnp.take(orbitals, band_ranking[0, :GB], axis=0).astype(jnp.float32)
    states = jnp.take(pool_states, state_order[:NQ], axis=0).astype(jnp.float32)
    density = (window[:, None] * states[None]).astype(jnp.bfloat16)
    density = density.reshape(pair_count, x_local, y_local, NZ)
    received = lax.all_to_all(density, ("row", "col"), split_axis=0, concat_axis=0, tiled=True)
    received = received.reshape(row_devices, col_devices, per_device, x_local, y_local, NZ)
    y_table = complex_table(NY).reshape(2, 2, col_devices, y_local, NY)
    x_table = complex_table(NX).reshape(2, 2, row_devices, x_local, NX)
    grid_field = jnp.einsum(
        "rcpxyz,bzk->bprcxyk", received.astype(jnp.float32), real_table(NZ), precision=accurate
    )
    grid_field = jnp.einsum("aprcxyz,abcyw->bprxwz", grid_field, y_table, precision=accurate)
    grid_field = jnp.einsum("aprxwz,abrxv->pbvwz", grid_field, x_table, precision=accurate)
    flat_field = grid_field.reshape(per_device, 2, NX * NY * NZ)
    picked = jnp.take(flat_field, gvector_index, axis=2) * (1.0 / math.sqrt(NX * NY * NZ))
    own_pairs = picked.astype(jnp.bfloat16)
    fanned = lax.all_gather(own_pairs, "col", axis=0, tiled=True)
    rows_all = lax.all_to_all(fanned, ("band", "row"), split_axis=2, concat_axis=0, tiled=True)
    col_width = screened.shape[2]
    own_columns = lax.dynamic_slice_in_dim(fanned, lax.axis_index("col") * col_width, col_width, 2)
    window_bands = lax.axis_size("band") * GB
    local_count = own_columns.shape[0]
    products = lax.dot_general(
        rows_all, screened, (((2,), (1,)), ((), ())), preferred_element_type=jnp.float32
    )
    left_pairs = lax.psum_scatter(
        jnp.stack(
            [products[:, 0, 0] + products[:, 1, 1], products[:, 0, 1] - products[:, 1, 0]], axis=1
        ),
        ("band", "row"),
        scatter_dimension=0,
        tiled=True,
    )
    local_bands = local_count // NQ
    left_pairs = left_pairs.reshape(local_bands, NQ, 2, col_width)
    right_pairs = own_columns.astype(jnp.float32).reshape(local_bands, NQ, 2, col_width)
    local_sigma = quadratic(left_pairs, right_pairs, -1.0, 1.0)
    offset = lax.axis_index(("band", "row")) * local_bands
    empty = jnp.zeros((2, NQ, NQ, window_bands), jnp.float32)
    partial_sigma = lax.dynamic_update_slice(
        empty, local_sigma, (jnp.int32(0), jnp.int32(0), jnp.int32(0), offset)
    )
    return lax.psum(partial_sigma, ("band", "row", "col"))


def solution(mesh):
    placed = (
        P("band", "row", "col", None),
        P("band", None),
        P(None, "row", "col", None),
        P(),
        P(),
        P(None, ("band", "row"), "col"),
    )
    return jax.shard_map(body, mesh=mesh, in_specs=placed, out_specs=P(), check_vma=False)
```

profile of v0, /device:TPU:0, one launch (start us, length us, event | category | flops | bytes accessed | tf_op | source)
XLA Modules:
  0.0 640.6 jit_solution(17084512975711009780)
XLA Ops:
  6.5 0.0 copy-start
  6.5 0.8 fusion.44
  7.3 0.7 compare_and_fusion.2
  8.0 0.7 compare_and_fusion.1
  8.7 1.6 gather_fusion.1
  10.3 0.1 select_convert_fusion.1
  10.4 0.0 copy-done
  10.4 0.7 gather_fusion
  11.2 0.2 select_convert_fusion
  11.4 0.0 copy-start.2
  11.4 1.9 multiply_convert_fusion
  13.3 7.4 %all-to-all-start = ((bf16[32,16,16,128]{3,2,1,0:T(8,128)(2,1)}), bf16[32,16,16,128]{3,2,1,0:T(8,128)(2,1)S(1)}, u32[]{:S(2)}, u32[]{:S(2)}) async-start(bf16[32,16,16,128]{3,2,1,0:T(8,128)(2,1)} %bitcast.9), calls=%async_computation | async-start | bytes 4194304 | tf_op jit(solution)/shard_map/all_to_all | solution.py:62
  20.7 0.0 reduce-scatter.2.cloned.1.call-start
  20.7 0.3 sine_negate_fusion
  21.0 0.2 fusion.43
  21.2 0.0 copy-done.2
  21.3 48.8 %all-to-all-done = bf16[32,16,16,128]{3,2,1,0:T(8,128)(2,1)S(1)} async-done(((bf16[32,16,16,128]{3,2,1,0:T(8,128)(2,1)}), bf16[32,16,16,128]{3,2,1,0:T(8,128)(2,1)S(1)}, u32[]{:S(2)}, u32[]{:S(2)}) %all-to-all-start) | async-done | bytes 2097184 | tf_op jit(solution)/shard_map/all_to_all | solution.py:62
  70.1 2.3 convolution_bitcast_fusion
  72.4 4.3 fusion.8
  76.8 8.6 %fusion.11 = f32[2,2,64,64,128]{4,2,3,0,1:T(8,128)S(1)} fusion(f32[2,2,4,16,64,128]{5,4,3,2,1,0:T(8,128)S(1)} %fusion.8, f32[1,1,4,16,64]{4,3,2,0,1:T(8,128)S(1)} %get-tuple-element.13, f32[1,1,4,16,64]{4,3,2,0,1:T(8,128)S(1)} %get-tuple-element.12, f32[1,1,4,16,64]{4,3,2,0,1:T(8,128)S(1)} %get-tuple-element.11), kind=kOutput, calls=%fused_computation.14 | convolution fusion | flops 1610661888 | bytes 16826368 | tf_op jit(solution)/shard_map/aprxwz,abrxv->pbvwz/dot_general | solution.py:70
  85.3 8.1 %copy.24 = f32[2,2,64,64,128]{4,3,2,1,0:T(8,128)} copy(f32[2,2,64,64,128]{4,2,3,0,1:T(8,128)S(1)} %fusion.11) | data formatting | bytes 16777216 | tf_op jit(solution)/shard_map/aprxwz,abrxv->pbvwz/transpose | solution.py:70
  93.4 9.5 %reshape.271 = f32[2,2,524288]{2,1,0:T(2,128)} reshape(f32[2,2,64,64,128]{4,3,2,1,0:T(8,128)} %copy.24) | data formatting | bytes 16777216 | tf_op jit(solution)/shard_map/reshape | solution.py:71
  102.9 301.2 %gather_fusion.2 = f32[24576,2,2]{0,2,1:T(2,128)S(1)} fusion(f32[2,2,524288]{2,1,0:T(2,128)} %reshape.271, s32[24576]{0:T(1024)S(1)} %fusion.27), kind=kCustom, calls=%fused_computation.2 | custom fusion | bytes 884736 | tf_op jit(solution)/shard_map/jit(_take)/gather | solution.py:72
  404.1 0.3 fusion.20
  404.4 18.2 %all_gather.3 = bf16[8,2,24576]{2,1,0:T(2,128)(2,1)S(1)} all-gather(bf16[2,2,24576]{2,1,0:T(2,128)(2,1)S(1)} %fusion.20), channel_id=1, replica_groups=mesh['band'=2,'row'=4,'col'=4] {'col'}, dimensions={0}, use_global_device_ids=true | all-gather | bytes 983040 | tf_op jit(solution)/shard_map/all_gather | solution.py:74
  422.6 19.3 %copy.26 = bf16[8,2,24576]{0,1,2:T(2,128)(2,1)} copy(bf16[8,2,24576]{2,1,0:T(2,128)(2,1)S(1)} %all_gather.3) | data formatting | bytes 1572864 | tf_op jit(solution)/shard_map/all_gather | solution.py:74
  441.9 15.0 %reshape.310 = bf16[8,2,24576]{2,1,0:T(2,128)(2,1)S(1)} reshape(bf16[24576,2,8]{2,1,0:T(2,128)(2,1)} %bitcast.99) | data formatting | bytes 1572864
  456.9 15.4 %all_to_all.23 = bf16[8,2,24576]{2,1,0:T(2,128)(2,1)S(1)} all-to-all(bf16[8,2,24576]{2,1,0:T(2,128)(2,1)S(1)} %reshape.310), channel_id=1, replica_groups=mesh['band'=2,'row'=4,'col'=4] {'band','row'}, dimensions={0} | all-to-all | bytes 1572864 | tf_op jit(solution)/shard_map/all_to_all | solution.py:75
  472.3 15.5 %reshape.311 = bf16[24576,2,8]{2,1,0:T(2,128)(2,1)} reshape(bf16[8,2,24576]{2,1,0:T(2,128)(2,1)S(1)} %all_to_all.23) | data formatting | bytes 1572864
  487.8 23.4 %copy.27 = bf16[8,2,8,3072]{3,0,2,1:T(8,128)(2,1)S(1)} copy(bf16[8,2,8,3072]{0,1,3,2:T(2,128)(2,1)} %bitcast.98) | data formatting | bytes 1572864 | tf_op jit(solution)/shard_map/all_to_all | solution.py:75
  511.2 28.1 %fusion = f32[64,2,2,6144]{3,0,2,1:T(8,128)} fusion(bf16[2,3072,6144]{2,1,0:T(8,128)(2,1)} %param.11, bf16[8,2,8,3072]{3,0,2,1:T(8,128)(2,1)S(1)} %copy.27), kind=kOutput, calls=%fused_computation.3 | convolution fusion | flops 9663676416 | bytes 82575360 | tf_op jit(solution)/shard_map/dot_general | solution.py:80
  539.3 3.2 fusion.15
  542.5 1.9 pad_maximum_fusion
  544.4 0.0 copy-start.1
  544.4 0.0 reduce-scatter.2.cloned.1.call-update
  544.4 0.1 constant_dynamic-slice_fusion
  544.6 0.3 fusion.48
  544.9 43.9 %reduce-scatter.2.cloned.1.call-done = f32[8,2,6144]{2,0,1:T(8,128)} async-done(((f32[64,2,6144]{2,0,1:T(8,128)}), f32[8,2,6144]{2,0,1:T(8,128)}) %reduce-scatter.2.cloned.1.call-update) | async-done | bytes 393232 | tf_op jit(solution)/shard_map/reduce_scatter | solution.py:83
  588.8 1.2 reshape.273
  590.0 0.9 fusion.22
  590.9 0.9 fusion.21
  591.8 0.9 fusion.18
  592.7 0.1 copy.28
  592.8 0.8 fusion.16
  593.6 0.1 copy.29
  593.7 0.2 dynamic_update_slice.3
  593.9 39.9 %psum.7 = f32[2,2,2,32]{3,2,1,0:T(2,128)} all-reduce(f32[2,2,2,32]{3,2,1,0:T(2,128)S(1)} %dynamic_update_slice.3), channel_id=1, replica_groups=mesh['band'=2,'row'=4,'col'=4] {'band','row','col'}, use_global_device_ids=true, to_apply=%region_1.2 | all-reduce | flops 256 | bytes 2048 | tf_op jit(solution)/shard_map/psum | solution.py:100
  633.7 0.0 copy-done.1
  (7 shorter events, 0.1 us)
Async XLA Ops:
  6.5 3.9 copy-start
  11.4 9.9 %copy-start.2 = (s32[24576]{0:T(1024)S(1)}, s32[24576]{0:T(1024)}, u32[]{:S(2)}) copy-start(s32[24576]{0:T(1024)} %param.10) | copy-start | bytes 294916
  13.3 56.8 %all-to-all-start = ((bf16[32,16,16,128]{3,2,1,0:T(8,128)(2,1)}), bf16[32,16,16,128]{3,2,1,0:T(8,128)(2,1)S(1)}, u32[]{:S(2)}, u32[]{:S(2)}) async-start(bf16[32,16,16,128]{3,2,1,0:T(8,128)(2,1)} %bitcast.9), calls=%async_computation | async-start | bytes 4194304 | tf_op jit(solution)/shard_map/all_to_all | solution.py:62
  20.7 568.1 %reduce-scatter.2.cloned.1.call-start = ((), (), s32[]{:S(2)}) async-start(), calls=%async_computation.3 | async-start | bytes 3538944 | tf_op jit(solution)/shard_map/reduce_scatter | solution.py:83
  544.4 89.3 %copy-start.1 = (bf16[32,16,16,128]{3,2,1,0:T(8,128)(2,1)S(1)}, bf16[32,16,16,128]{3,2,1,0:T(8,128)(2,1)}, u32[]{:S(2)}) copy-start(bf16[32,16,16,128]{3,2,1,0:T(8,128)(2,1)} %param.6) | copy-start | bytes 6291460
Sparse Core Ops, SparseCore 0:
  544.6 44.1 reduce-scatter.1
where the time goes:
time: 648 us; the launch traced here: 641 us
  local copies, waits for them, and re-layouts  396 us (61%)
  waiting for transfers between devices  92.7 us (14%)
  blocking collectives  73.4 us (11%)
  matrix products  46.7 us (7%)
  between operations  13.6 us (2%)
  other arithmetic  10.4 us (2%)
  starting transfers between devices  7.4 us (1%)
    gather x1, local copies, waits for them, and re-layouts, body(): jnp.take(flat_field, gvector_index, axis=2)  301 us
    all_to_all x1, waiting for transfers between devices, body(): lax.all_to_all(density, ('row', 'col'), split_axis=0, concat_axis=0, tile...  48.8 us
    reduce_scatter x1, waiting for transfers between devices, body(): lax.psum_scatter(jnp.stack([products[:, 0, 0] + products[:, 1, 1], produc...  43.9 us
    psum x1, blocking collectives, body(): return lax.psum(partial_sigma, ('band', 'row', 'col'))  39.9 us
    unnamed x8, local copies, waits for them, and re-layouts  30.6 us
    dot_general x1, matrix products, body(): lax.dot_general(rows_all, screened, (((2,), (1,)), ((), ())), preferred_e...  28.1 us
    all_to_all x1, local copies, waits for them, and re-layouts, body(): lax.all_to_all(fanned, ('band', 'row'), split_axis=2, concat_axis=0, tile...  23.4 us
    all_gather x1, local copies, waits for them, and re-layouts, body(): fanned = lax.all_gather(own_pairs, 'col', axis=0, tiled=True)  19.3 us
  transfers between devices with their start and end apart: 2, of which 2 were waited for; matrix products, arithmetic and copies ran while one was open for 0% of the time, Pallas kernels for 0%

commit v1 on v0

v1 whole, which is shorter than its diff:
```python
import functools
import math

import jax
import jax.numpy as jnp
import numpy as np
from jax import lax
from jax.experimental import pallas as pl
from jax.experimental.pallas import tpu as pltpu
from jax.sharding import PartitionSpec as P

NX = 64
NY = 64
NZ = 128
GB = 16
NQ = 2
LANES = 128
SUBS = 8
COMPS = 4


def angles(length):
    indices = np.arange(length)
    return (indices[:, None] * indices[None, :] % length) * (2.0 * math.pi / length)


def real_table(length):
    turn = angles(length)
    return np.stack([np.cos(turn), -np.sin(turn)]).astype(np.float32)


def complex_table(length):
    turn = angles(length)
    cosine, sine = np.cos(turn), np.sin(turn)
    return np.stack([np.stack([cosine, -sine]), np.stack([sine, cosine])]).astype(np.float32)


def x_matrix(per_device):
    table = complex_table(NX).astype(np.float64) / math.sqrt(NX * NY * NZ)
    full = np.zeros((NX, COMPS, per_device, 2, NX), np.float64)
    for pair in range(per_device):
        for out in range(2):
            for part in range(2):
                full[:, 2 * pair + out, pair, part, :] = table[part, out].T
    return full.reshape(NX * COMPS, per_device * 2 * NX).astype(np.float32)


def split(value):
    high = value.astype(jnp.bfloat16)
    return high, (value - high.astype(jnp.float32)).astype(jnp.bfloat16)


def density_kernel(ranking_ref, order_ref, orbitals_ref, pool_ref, out_ref):
    def band(j, carry):
        orbital = orbitals_ref[ranking_ref[0, j]].astype(jnp.float32)
        for n in range(NQ):
            state = pool_ref[order_ref[n]].astype(jnp.float32)
            out_ref[j, n] = (orbital * state).astype(jnp.bfloat16)
        return carry

    lax.fori_loop(0, out_ref.shape[0], band, 0)


def densities(orbitals, band_ranking, pool_states, state_order):
    smem = pl.BlockSpec(memory_space=pltpu.SMEM)
    vmem = pl.BlockSpec(memory_space=pltpu.VMEM)
    return pl.pallas_call(
        density_kernel,
        out_shape=jax.ShapeDtypeStruct((GB, NQ) + orbitals.shape[1:], jnp.bfloat16),
        in_specs=[smem, smem, vmem, vmem],
        out_specs=vmem,
        compiler_params=pltpu.CompilerParams(vmem_limit_bytes=32 * 1024 * 1024),
    )(band_ranking, state_order, orbitals, pool_states)


def pick_kernel(row_ref, turn_ref, high_ref, low_ref, field_ref, out_ref, table, picked):
    def mm(a, b):
        return jnp.dot(a, b, preferred_element_type=jnp.float32)

    def transform(w, carry):
        data_high, data_low = split(field_ref[w])
        value = mm(high_ref[...], data_high) + (
            mm(high_ref[...], data_low) + mm(low_ref[...], data_high)
        )
        table[pl.ds(w * NX, NX)] = value.reshape(NX, COMPS, LANES)
        return carry

    lax.fori_loop(0, NY, transform, 0)
    lane = lax.broadcasted_iota(jnp.int32, (COMPS, LANES), 1)

    def block(b, carry):
        held = [jnp.zeros((COMPS, LANES), jnp.float32) for _ in range(4)]
        base = b * LANES
        for j in range(LANES):
            row = table[row_ref[base + j]]
            held[j % 4] = jnp.where(
                lane == j, pltpu.roll(row, turn_ref[base + j], 1), held[j % 4]
            )
        total = (held[0] + held[1]) + (held[2] + held[3])
        picked[b] = total
        return carry

    lax.fori_loop(0, picked.shape[0], block, 0)
    for c in range(out_ref.shape[0]):
        out_ref[c] = picked[:, c, :].astype(jnp.bfloat16)


def pick(field, gvector_index, per_device):
    count = gvector_index.shape[0]
    rows = (gvector_index // NZ) % NY * NX + gvector_index // (NY * NZ)
    turns = (jnp.arange(count, dtype=jnp.int32) - gvector_index % NZ) % LANES
    high, low = split(jnp.asarray(x_matrix(per_device)))
    smem = pl.BlockSpec(memory_space=pltpu.SMEM)
    vmem = pl.BlockSpec(memory_space=pltpu.VMEM)
    return pl.pallas_call(
        pick_kernel,
        out_shape=jax.ShapeDtypeStruct((2 * per_device, count // LANES, LANES), jnp.bfloat16),
        in_specs=[smem, smem, vmem, vmem, vmem],
        out_specs=vmem,
        scratch_shapes=[
            pltpu.VMEM((NX * NY, COMPS, LANES), jnp.float32),
            pltpu.VMEM((count // LANES, COMPS, LANES), jnp.float32),
        ],
        compiler_params=pltpu.CompilerParams(vmem_limit_bytes=56 * 1024 * 1024),
    )(rows, turns, high, low, field)


def swap_matrix(bands):
    full = np.zeros((SUBS, bands, bands, SUBS), np.float32)
    for s in range(SUBS):
        for m in range(bands):
            full[s, m, m, s] = 1.0
    return full.reshape(SUBS * bands, bands * SUBS)


def sigma_kernel(group, swap_ref, rows_ref, cols_ref, tile_ref, out_ref, left, right, total):
    step = pl.program_id(0)
    bands = rows_ref.shape[0]
    width = tile_ref.shape[2]

    @pl.when(step == 0)
    def _():
        total[...] = jnp.zeros_like(total)
        for source, target in ((rows_ref, left), (cols_ref, right)):
            for part in range(2):
                for n in range(NQ):
                    for m in range(0, bands, group):
                        first = (part * NQ + n) * bands + m

                        def move(s, carry):
                            rows = pl.ds(pl.multiple_of(s * SUBS, SUBS), SUBS)
                            data = source[m : m + group, n, part, rows, :].astype(jnp.float32)
                            data = data.reshape(group * SUBS, LANES).astype(jnp.bfloat16)
                            data = jnp.dot(
                                swap_ref[...], data, preferred_element_type=jnp.float32
                            ).astype(jnp.bfloat16)
                            for k in range(SUBS):
                                lanes = pl.ds(
                                    pl.multiple_of((s * SUBS + k) * LANES, LANES), LANES
                                )
                                target[first : first + group, lanes] = data[
                                    k * group : (k + 1) * group
                                ]
                            return carry

                        lax.fori_loop(0, source.shape[3] // SUBS, move, 0)

    depth = tile_ref.shape[1]
    half = NQ * bands
    a = jnp.dot(left[:, :depth], tile_ref[0], preferred_element_type=jnp.float32)
    b = jnp.dot(left[:, :depth], tile_ref[1], preferred_element_type=jnp.float32)
    real = a[:half] + b[half:]
    imag = b[:half] - a[half:]
    lanes = pl.ds(pl.multiple_of(step * width, width), width)
    other = right[:, lanes].astype(jnp.float32)
    for n in range(NQ):
        lr = real[n * bands : (n + 1) * bands]
        li = imag[n * bands : (n + 1) * bands]
        for k in range(NQ):
            qr = other[k * bands : (k + 1) * bands]
            qi = other[half + k * bands : half + (k + 1) * bands]
            re = lr * qr - li * qi
            im = lr * qi + li * qr
            for part, value in ((0, re), (1, im)):
                held = total[part, n, k]
                for piece in range(width // LANES):
                    held = held + value[:, piece * LANES : (piece + 1) * LANES]
                total[part, n, k] = held

    @pl.when(step == pl.num_programs(0) - 1)
    def _():
        out_ref[...] = total[...]


def sigma_tile(rows, cols, screened):
    bands = rows.shape[0]
    group = 32
    width = 512
    depth, columns = screened.shape[1:]
    extra = -rows.shape[3] % SUBS
    if extra:
        rows = jnp.pad(rows, ((0, 0),) * 3 + ((0, extra), (0, 0)))
    swap = jnp.asarray(swap_matrix(group)).astype(jnp.bfloat16)
    whole = pl.BlockSpec(memory_space=pltpu.VMEM)
    return pl.pallas_call(
        functools.partial(sigma_kernel, group),
        grid=(columns // width,),
        out_shape=jax.ShapeDtypeStruct((2, NQ, NQ, bands, LANES), jnp.float32),
        in_specs=[whole, whole, whole, pl.BlockSpec((2, depth, width), lambda i: (0, 0, i))],
        out_specs=pl.BlockSpec((2, NQ, NQ, bands, LANES), lambda i: (0, 0, 0, 0, 0)),
        scratch_shapes=[
            pltpu.VMEM((2 * NQ * bands, rows.shape[3] * LANES), jnp.bfloat16),
            pltpu.VMEM((2 * NQ * bands, columns), jnp.bfloat16),
            pltpu.VMEM((2, NQ, NQ, bands, LANES), jnp.float32),
        ],
        compiler_params=pltpu.CompilerParams(vmem_limit_bytes=56 * 1024 * 1024),
    )(swap, rows, cols, screened)


def body(orbitals, band_ranking, pool_states, state_order, gvector_index, screened):
    accurate = lax.Precision.HIGH
    x_local = orbitals.shape[1]
    y_local = orbitals.shape[2]
    row_devices = lax.axis_size("row")
    col_devices = lax.axis_size("col")
    band_devices = lax.axis_size("band")
    pair_count = GB * NQ
    per_device = pair_count // (row_devices * col_devices)
    density = densities(orbitals, band_ranking, pool_states, state_order)
    density = density.reshape(pair_count, x_local, y_local, NZ)
    received = lax.all_to_all(density, ("row", "col"), split_axis=0, concat_axis=0, tiled=True)
    received = received.reshape(row_devices, col_devices, per_device, x_local, y_local, NZ)
    y_table = jnp.asarray(complex_table(NY)).reshape(2, 2, col_devices, y_local, NY)
    z_table = jnp.asarray(real_table(NZ))
    field = jnp.einsum(
        "rcpxyz,bzk->bprcxyk", received.astype(jnp.float32), z_table, precision=accurate
    )
    field = jnp.einsum("aprcxyz,abcyw->wpbrxz", field, y_table, precision=accurate)
    field = field.reshape(NY, per_device * 2 * NX, NZ)
    own = pick(field, gvector_index, per_device)

    own = own.reshape(per_device, 2, -1, LANES)
    others = band_devices * row_devices
    by_col = own.reshape(per_device, 2, col_devices, -1, LANES)
    by_col = lax.all_to_all(by_col, "col", split_axis=2, concat_axis=0, tiled=False)
    cols = lax.all_gather(by_col, ("band", "row"), axis=0, tiled=False)
    by_row = own.reshape(per_device, 2, others, -1, LANES)
    by_row = lax.all_to_all(by_row, ("band", "row"), split_axis=2, concat_axis=0, tiled=False)
    rows = lax.all_gather(by_row, "col", axis=1, tiled=False)
    bands = band_devices * GB
    cols = cols.reshape(bands, NQ, 2, -1, LANES)
    rows = rows.reshape(bands, NQ, 2, -1, LANES)
    share = jnp.sum(sigma_tile(rows, cols, screened), axis=-1)
    shares = lax.all_gather(share, ("band", "row", "col"), axis=0, tiled=False)
    return jnp.sum(shares, axis=0)


def solution(mesh):
    placed = (
        P("band", "row", "col", None),
        P("band", None),
        P(None, "row", "col", None),
        P(),
        P(),
        P(None, ("band", "row"), "col"),
    )
    return jax.shard_map(body, mesh=mesh, in_specs=placed, out_specs=P(), check_vma=False)
```

time: 648 us -> 306 us (0.47); the launches traced: 641 us -> 306 us
  local copies, waits for them, and re-layouts: 396 us -> 14.9 us
  Pallas kernels: 0 us -> 110 us
  waiting for transfers between devices: 92.7 us -> 48.5 us
  matrix products: 46.7 us -> 6.12 us
  blocking collectives: 73.4 us -> 103 us
  other arithmetic: 10.4 us -> 2.56 us
    gather x3 -> x0, local copies, waits for them, and re-layouts: 304 us -> none  [the longest x1 301 us: body(): jnp.take(flat_field, gvector_index, axis=2)]
    pallas_call x0 -> x3, Pallas kernels: none -> 110 us  [the longest x1 73 us: pick(): pl.pallas_call(pick_kernel, out_shape=jax.ShapeDtypeStruct((2 * per_devic...]
    all_gather x1 -> x2, blocking collectives: 18.2 us -> 82 us  [the longest x1 64.4 us: body(): shares = lax.all_gather(share, ('band', 'row', 'col'), axis=0, tiled=False)]
    reduce_scatter x1 -> x0, waiting for transfers between devices: 43.9 us -> none  [body(): lax.psum_scatter(jnp.stack([products[:, 0, 0] + products[:, 1, 1], produc...]
    dot_general x8 -> x2, matrix products: 46.7 us -> 6.12 us  [the longest x1 3.8 us: body(): jnp.einsum('aprcxyz,abcyw->wpbrxz', field, y_table, precision=accurate)]
    psum x1 -> x0, blocking collectives: 39.9 us -> none  [body(): return lax.psum(partial_sigma, ('band', 'row', 'col'))]
    unnamed x8 -> x14, local copies, waits for them, and re-layouts: 30.6 us -> 3.95 us
    all_to_all x1 -> x0, local copies, waits for them, and re-layouts: 23.4 us -> none  [body(): lax.all_to_all(fanned, ('band', 'row'), split_axis=2, concat_axis=0, tile...]
  transfers between devices with their start and end apart: 2 -> 2, of which waited for: 2 -> 1; matrix products, arithmetic and copies ran while one was open for 0% -> 1% of each run, Pallas kernels for 0% -> 0%
where the time goes in v1:
time: 306 us
  Pallas kernels  110 us (36%)
  blocking collectives  103 us (34%)
  waiting for transfers between devices  48.5 us (16%)
  local copies, waits for them, and re-layouts  14.9 us (5%)
  between operations  13.5 us (4%)
  starting transfers between devices  7.53 us (2%)
  matrix products  6.12 us (2%)
    pallas_call x1, Pallas kernels, pick(): pl.pallas_call(pick_kernel, out_shape=jax.ShapeDtypeStruct((2 * per_devic...  73 us
    all_gather x1, blocking collectives, body(): shares = lax.all_gather(share, ('band', 'row', 'col'), axis=0, tiled=False)  64.4 us
    all_to_all x1, waiting for transfers between devices, body(): lax.all_to_all(density, ('row', 'col'), split_axis=0, concat_axis=0, tile...  48.5 us
    pallas_call x1, Pallas kernels, sigma_tile(): pl.pallas_call(functools.partial(sigma_kernel, group), grid=(columns // w...  34.1 us
    all_gather x1, blocking collectives, body(): rows = lax.all_gather(by_row, 'col', axis=1, tiled=False)  17.7 us
    all_to_all x1, blocking collectives, body(): lax.all_to_all(by_col, 'col', split_axis=2, concat_axis=0, tiled=False)  10.7 us
    all_to_all x1, blocking collectives, body(): lax.all_to_all(by_row, ('band', 'row'), split_axis=2, concat_axis=0, tile...  10.4 us
    transpose x1, local copies, waits for them, and re-layouts, body(): jnp.einsum('aprcxyz,abcyw->wpbrxz', field, y_table, precision=accurate)  8.09 us
  transfers between devices with their start and end apart: 2, of which 1 were waited for; matrix products, arithmetic and copies ran while one was open for 1% of the time, Pallas kernels for 0%

profile of v1, /device:TPU:0, one launch (start us, length us, event | category | flops | bytes accessed | tf_op | source)
XLA Modules:
  0.0 305.7 jit_solution(9056234866070078446)
XLA Ops:
  6.5 0.0 copy-start
  6.5 1.6 copy-done
  8.1 0.0 copy-start.1
  8.1 1.0 copy-done.1
  9.2 0.0 copy-start.2
  9.2 0.7 copy-done.2
  9.8 0.0 copy-start.3
  9.8 0.7 copy-done.3
  10.5 0.0 copy-start.6
  10.5 0.0 copy-start.5
  10.5 2.4 shard_map.100
  12.9 0.0 copy-start.4
  12.9 7.5 %all-to-all-start = ((bf16[32,16,16,128]{3,2,1,0:T(8,128)(2,1)}), bf16[32,16,16,128]{3,2,1,0:T(8,128)(2,1)S(1)}, u32[]{:S(2)}, u32[]{:S(2)}) async-start(bf16[32,16,16,128]{3,2,1,0:T(8,128)(2,1)} %bitcast), calls=%async_computation | async-start | bytes 4194304 | tf_op jit(solution)/shard_map/all_to_all | solution.py:231
  20.4 0.0 all-gather.5.cloned.1.call-start
  20.5 0.0 copy-done.6
  20.5 0.9 add_select_fusion
  21.3 48.5 %all-to-all-done = bf16[32,16,16,128]{3,2,1,0:T(8,128)(2,1)S(1)} async-done(((bf16[32,16,16,128]{3,2,1,0:T(8,128)(2,1)}), bf16[32,16,16,128]{3,2,1,0:T(8,128)(2,1)S(1)}, u32[]{:S(2)}, u32[]{:S(2)}) %all-to-all-start) | async-done | bytes 2097184 | tf_op jit(solution)/shard_map/all_to_all | solution.py:231
  69.8 0.0 copy-done.5
  69.8 2.3 fusion.5
  72.2 0.0 copy-done.4
  72.2 3.8 %fusion.2 = f32[64,2,2,4,16,128]{5,0,2,4,3,1:T(8,128)S(1)} fusion(f32[2,2,4,16,64,1,1,1]{4,3,2,0,1,7,6,5:T(8,128)S(1)} %copy-done.4, f32[4,4,2,16,16,2,128]{6,4,1,5,3,0,2:T(8,128)S(1)} %fusion.5), kind=kOutput, calls=%fused_computation.2 | convolution fusion | flops 1610612736 | bytes 16842752 | tf_op jit(solution)/shard_map/aprcxyz,abcyw->wpbrxz/dot_general | solution.py:238
  76.0 8.1 %copy.28 = f32[64,2,2,4,16,128]{5,4,3,2,1,0:T(8,128)} copy(f32[64,2,2,4,16,128]{5,0,2,4,3,1:T(8,128)S(1)} %fusion.2) | data formatting | bytes 16777216 | tf_op jit(solution)/shard_map/aprcxyz,abcyw->wpbrxz/transpose | solution.py:238
  84.1 73.0 %shard_map.101 = bf16[4,192,128]{2,1,0:T(8,128)(2,1)} custom-call(s32[24576]{0:T(1024)} %get-tuple-element.6.row_ref, s32[24576]{0:T(1024)} %get-tuple-element.5.turn_ref, bf16[256,256]{1,0:T(8,128)(2,1)} %constant.72.high_ref, bf16[256,256]{1,0:T(8,128)(2,1)} %constant.75.low_ref, f32[64,256,128]{2,1,0:T(8,128)} %bitcast.43), custom_call_target="tpu_custom_call" | custom-call | tf_op jit(solution)/shard_map/pallas_call | solution.py:115
  157.1 0.9 copy.32
  158.1 10.7 %all_to_all.35 = bf16[1,2,2,4,48,128]{5,4,2,1,0,3:T(8,128)(2,1)} all-to-all(bf16[1,2,2,4,48,128]{5,4,2,1,0,3:T(8,128)(2,1)S(1)} %copy.32), channel_id=1, replica_groups=mesh['band'=2,'row'=4,'col'=4] {'col'}, dimensions={3} | all-to-all | bytes 393216 | tf_op jit(solution)/shard_map/all_to_all | solution.py:245
  168.7 0.0 all-gather.5.cloned.1.call-update
  168.8 0.9 copy.29
  169.7 10.4 %all_to_all.36 = bf16[1,2,2,8,24,128]{5,4,2,1,0,3:T(8,128)(2,1)S(1)} all-to-all(bf16[1,2,2,8,24,128]{5,4,2,1,0,3:T(8,128)(2,1)S(1)} %copy.29), channel_id=1, replica_groups=mesh['band'=2,'row'=4,'col'=4] {'band','row'}, dimensions={3} | all-to-all | bytes 393216 | tf_op jit(solution)/shard_map/all_to_all | solution.py:248
  180.1 17.7 %all-gather = bf16[8,4,2,2,1,24,128]{6,5,4,3,2,0,1:T(8,128)(2,1)S(1)} all-gather(bf16[8,1,2,2,1,24,128]{6,5,4,3,2,0,1:T(8,128)(2,1)S(1)} %bitcast.50), channel_id=2, replica_groups=mesh['band'=2,'row'=4,'col'=4] {'col'}, dimensions={1}, use_global_device_ids=true | all-gather | bytes 983040 | tf_op jit(solution)/shard_map/all_gather | solution.py:249
  197.8 1.0 copy.31
  198.7 0.0 all-gather.5.cloned.1.call-done
  198.7 34.1 %shard_map.102 = f32[2,2,2,32,128]{4,3,2,1,0:T(8,128)} custom-call(bf16[256,256]{1,0:T(8,128)(2,1)} %constant.71.swap_ref, bf16[32,2,2,24,128]{4,3,2,1,0:T(8,128)(2,1)} %bitcast.45, bf16[32,2,2,48,128]{4,3,2,1,0:T(8,128)(2,1)} %bitcast.48, bf16[2,3072,6144]{2,1,0:T(8,128)(2,1)} %tile_ref.1), custom_call_target="tpu_custom_call" | custom-call | tf_op jit(solution)/shard_map/pallas_call | solution.py:205
  232.8 1.0 reduce_sum.18
  233.8 64.4 %all-gather.2 = f32[64,2,2,32]{3,2,1,0:T(2,128)S(1)} all-gather(f32[2,2,2,32]{3,2,1,0:T(2,128)S(1)} %reduce_sum.18), channel_id=4, replica_groups=mesh['band'=2,'row'=4,'col'=4] {'band','row','col'}, dimensions={0}, use_global_device_ids=true | all-gather | bytes 33792 | tf_op jit(solution)/shard_map/all_gather | solution.py:254
  298.2 0.7 reduce_sum.19
Async XLA Ops:
  6.5 1.6 copy-start
  8.1 1.0 copy-start.1
  9.2 0.7 copy-start.2
  9.8 0.7 copy-start.3
  10.5 10.0 %copy-start.6 = (s32[24576]{0:T(1024)S(1)}, s32[24576]{0:T(1024)}, u32[]{:S(2)}) copy-start(s32[24576]{0:T(1024)} %param.14) | copy-start | bytes 294916
  10.5 59.4 %copy-start.5 = (f32[2,128,128,1,1,1,1]{2,1,4,0,6,3,5:T(8,128)S(1)}, f32[2,128,128,1,1,1,1]{2,1,4,0,6,3,5:T(8,128)}, u32[]{:S(2)}) copy-start(f32[2,128,128,1,1,1,1]{2,1,4,0,6,3,5:T(8,128)} %constant.77) | copy-start | bytes 393220
  12.9 59.3 %copy-start.4 = (f32[2,2,4,16,64,1,1,1]{4,3,2,0,1,7,6,5:T(8,128)S(1)}, f32[2,2,4,16,64,1,1,1]{4,3,2,0,1,7,6,5:T(8,128)}, u32[]{:S(2)}) copy-start(f32[2,2,4,16,64,1,1,1]{4,3,2,0,1,7,6,5:T(8,128)} %constant.78) | copy-start | bytes 196612
  12.9 56.9 %all-to-all-start = ((bf16[32,16,16,128]{3,2,1,0:T(8,128)(2,1)}), bf16[32,16,16,128]{3,2,1,0:T(8,128)(2,1)S(1)}, u32[]{:S(2)}, u32[]{:S(2)}) async-start(bf16[32,16,16,128]{3,2,1,0:T(8,128)(2,1)} %bitcast), calls=%async_computation | async-start | bytes 4194304 | tf_op jit(solution)/shard_map/all_to_all | solution.py:231
  20.4 178.3 %all-gather.5.cloned.1.call-start = ((), (), s32[]{:S(2)}) async-start(), calls=%async_computation.3 | async-start | bytes 1769472 | tf_op jit(solution)/shard_map/all_gather | solution.py:246
Sparse Core Ops, SparseCore 0:
  168.9 24.4 all-gather.4
